TPU v7x, 32 devices: a whole 2x2x4 slice. The times are simulated.
32 devices in a mesh: groups: 2 (over x), graph: 16 (over z, y, core).
Axes of the slice: x: 2, y: 2, z: 4, core: 2. Of those that a mesh axis runs over, the one named last changes fastest.
Arguments:
- node_feat: bfloat16 [8192, 512], P(('groups', 'graph')), parts along dimension 0, may hold values from -6 to 6
- edge_feat: bfloat16 [12288, 512], P(('groups', 'graph')), parts along dimension 0, may hold values from -6 to 6
- edge_source: int32 [12288], P(('groups', 'graph')), parts along dimension 0, may hold values from 0 to 383
- edge_target: int32 [12288], P(('groups', 'graph')), parts along dimension 0, may hold values from 0 to 255
- halo_rows: int32 [32, 16, 8], P(('groups', 'graph')), parts along dimension 0, may hold values from 0 to 255
- edge_count: int32 [32], P(('groups', 'graph')), parts along dimension 0, may hold values from 1 to 384, 3840 in all
- edge_w1: bfloat16 [1536, 512], replicated, may hold values from -0.15625 to 0.15625
- edge_b1: float32 [512], replicated, may hold values from -3 to 3
- edge_w2: bfloat16 [512, 512], replicated, may hold values from -0.25 to 0.25
- edge_gain: float32 [512], replicated, may hold values from 0.25 to 1.75
- node_w1: bfloat16 [1024, 512], replicated, may hold values from -0.1875 to 0.1875
- node_b1: float32 [512], replicated, may hold values from -3 to 3
- node_w2: bfloat16 [512, 512], replicated, may hold values from -0.25 to 0.25
- node_gain: float32 [512], replicated, may hold values from 0.25 to 1.75
- node_cot: bfloat16 [8192, 512], P(('groups', 'graph')), parts along dimension 0, may hold values from -6 to 6
- edge_cot: bfloat16 [12288, 512], P(('groups', 'graph')), parts along dimension 0, may hold values from -6 to 6
Outputs:
- node_out: bfloat16 [8192, 512], P(('groups', 'graph')), parts along dimension 0
- edge_out: bfloat16 [12288, 512], P(('groups', 'graph')), parts along dimension 0
- node_grad: float32 [8192, 512], P(('groups', 'graph')), parts along dimension 0
- edge_grad: float32 [12288, 512], P(('groups', 'graph')), parts along dimension 0
- grad_edge_w1: float32 [3072, 512], P(('groups', 'graph')), parts along dimension 0
- grad_edge_b1: float32 [1024], P(('groups', 'graph')), parts along dimension 0
- grad_edge_w2: float32 [1024, 512], P(('groups', 'graph')), parts along dimension 0
- grad_edge_gain: float32 [1024], P(('groups', 'graph')), parts along dimension 0
- grad_node_w1: float32 [2048, 512], P(('groups', 'graph')), parts along dimension 0
- grad_node_b1: float32 [1024], P(('groups', 'graph')), parts along dimension 0
- grad_node_w2: float32 [1024, 512], P(('groups', 'graph')), parts along dimension 0
- grad_node_gain: float32 [1024], P(('groups', 'graph')), parts along dimension 0
There are 2 independent parts, one for each index of `groups`. A program takes and returns all parts, laid end to end along the dimension named above; an argument that names none is the same for every part. Nothing has to cross between parts.
Inputs may be any that keep to these rules, and one draw needn't show every extreme that they name: halo_rows[q, p, k] is a row of partition q's own nodes that partition p receives in slot k; rows may repeat. `edge_source`: A value below 256 names an own node of the edge's partition; 256 + q * 8 + k names slot k of the rows received from partition q. `edge_target`: the receiver is an own node of the edge's partition. Partition p's first edge_count[p] edge slots are live, the rest padding; some partition has all 384 live.
All inputs are finite; a program needn't handle non-finite values. No bound on the sum of `edge_count` on one device may be relied on, other than what follows from the above.
Results may differ from a plain program's by a relative error of at most 0.009.
Values may be sent and summed in bfloat16 or wider, within the bound.
A program may use at most 128 MiB of HBM per device.

v0:
```python
import math

import jax
import jax.numpy as jnp
from jax import lax
from jax.sharding import PartitionSpec as P


def silu_grad(pre):
    sig = jax.nn.sigmoid(pre)
    return sig * (1.0 + pre * (1.0 - sig))


def layer_norm(values):
    centred = values - jnp.mean(values, axis=-1, keepdims=True)
    rstd = lax.rsqrt(jnp.mean(centred * centred, axis=-1, keepdims=True) + 1e-05)
    return (centred * rstd, rstd)


def mlp_forward(inputs, first, bias, second):
    pre = jnp.dot(inputs, first, preferred_element_type=jnp.float32) + bias
    active = jax.nn.silu(pre).astype(jnp.bfloat16)
    outer = jnp.dot(active, second, preferred_element_type=jnp.float32)
    normed, rstd = layer_norm(outer)
    return (pre, active, normed, rstd)


def mlp_backward(grad_branch, first, second, gain, pre, normed, rstd):
    grad_gain = jnp.sum(grad_branch * normed, axis=0)
    scaled = grad_branch * gain
    grad_outer = (
        scaled
        - jnp.mean(scaled, axis=-1, keepdims=True)
        - normed * jnp.mean(scaled * normed, axis=-1, keepdims=True)
    ) * rstd
    grad_outer = grad_outer.astype(jnp.bfloat16)
    grad_active = lax.dot_general(
        grad_outer, second, (((1,), (1,)), ((), ())), preferred_element_type=jnp.float32
    )
    grad_pre = (grad_active * silu_grad(pre)).astype(jnp.bfloat16)
    grad_bias = jnp.sum(grad_pre.astype(jnp.float32), axis=0)
    grad_inputs = lax.dot_general(
        grad_pre, first, (((1,), (1,)), ((), ())), preferred_element_type=jnp.float32
    )
    return (grad_inputs, grad_bias, grad_gain, grad_outer, grad_pre)


def transposed(left, right):
    return lax.dot_general(
        left, right, (((0,), (0,)), ((), ())), preferred_element_type=jnp.float32
    )


def indicator(index, count):
    return (index[:, None] == jnp.arange(count, dtype=jnp.int32)[None, :]).astype(jnp.bfloat16)


def on_device(
    node_feat,
    edge_feat,
    edge_source,
    edge_target,
    halo_rows,
    edge_count,
    edge_w1,
    edge_b1,
    edge_w2,
    edge_gain,
    node_w1,
    node_b1,
    node_w2,
    node_gain,
    node_cot,
    edge_cot,
):
    peers = lax.axis_size("graph")
    nodes_local, width = node_feat.shape
    edges_local = edge_feat.shape[0]
    slots = halo_rows.shape[2]
    table_rows = nodes_local + peers * slots
    requests = halo_rows.reshape(-1)
    outgoing = jnp.take(node_feat, requests, axis=0).reshape(peers, slots, width)
    received = lax.all_to_all(outgoing, "graph", split_axis=0, concat_axis=0, tiled=True)
    table = jnp.concatenate([node_feat, received.reshape(peers * slots, width)], axis=0)
    source_hot = indicator(edge_source, table_rows)
    target_hot = indicator(edge_target, nodes_local)
    senders = jnp.dot(source_hot, table, preferred_element_type=jnp.float32).astype(jnp.bfloat16)
    receivers = jnp.dot(target_hot, node_feat, preferred_element_type=jnp.float32).astype(
        jnp.bfloat16
    )
    live = (jnp.arange(edges_local, dtype=jnp.int32) < edge_count[0]).astype(jnp.float32)[:, None]
    edge_inputs = jnp.concatenate([edge_feat, senders, receivers], axis=1)
    pre_e, act_e, normed_e, rstd_e = mlp_forward(edge_inputs, edge_w1, edge_b1, edge_w2)
    message = (live * normed_e * edge_gain).astype(jnp.bfloat16)
    edge_out = (edge_feat.astype(jnp.float32) + message.astype(jnp.float32)).astype(jnp.bfloat16)
    agg = transposed(target_hot, message).astype(jnp.bfloat16)
    node_inputs = jnp.concatenate([node_feat, agg], axis=1)
    pre_n, act_n, normed_n, rstd_n = mlp_forward(node_inputs, node_w1, node_b1, node_w2)
    node_out = (node_feat.astype(jnp.float32) + normed_n * node_gain).astype(jnp.bfloat16)
    gin_n, gb_n, gg_n, gout_n, gpre_n = mlp_backward(
        node_cot.astype(jnp.float32), node_w1, node_w2, node_gain, pre_n, normed_n, rstd_n
    )
    grad_agg = gin_n[:, width:].astype(jnp.bfloat16)
    picked = jnp.dot(target_hot, grad_agg, preferred_element_type=jnp.float32)
    grad_message = edge_cot.astype(jnp.float32) + picked
    gin_e, gb_e, gg_e, gout_e, gpre_e = mlp_backward(
        grad_message * live, edge_w1, edge_w2, edge_gain, pre_e, normed_e, rstd_e
    )
    edge_grad = edge_cot.astype(jnp.float32) + gin_e[:, :width]
    grad_send = gin_e[:, width : 2 * width].astype(jnp.bfloat16)
    grad_recv = gin_e[:, 2 * width :].astype(jnp.bfloat16)
    table_grad = transposed(source_hot, grad_send)
    recv_grad = transposed(target_hot, grad_recv)
    halo_part = table_grad[nodes_local:].reshape(peers, slots, width)
    returned = lax.all_to_all(
        halo_part.astype(jnp.bfloat16), "graph", split_axis=0, concat_axis=0, tiled=True
    ).astype(halo_part.dtype)
    halo_grad = jax.ops.segment_sum(returned.reshape(peers * slots, width), requests, nodes_local)
    node_grad = (
        node_cot.astype(jnp.float32)
        + gin_n[:, :width]
        + table_grad[:nodes_local]
        + recv_grad
        + halo_grad
    )
    scale = 1.0 / math.sqrt(edges_local * peers)
    g_ew1, g_eb1, g_ew2, g_egain, g_nw1, g_nb1, g_nw2, g_ngain = (
        lax.psum_scatter(
            transposed(edge_inputs, gpre_e) * scale, "graph", scatter_dimension=0, tiled=True
        ),
        lax.psum_scatter(gb_e * scale, "graph", scatter_dimension=0, tiled=True),
        lax.psum_scatter(
            transposed(act_e, gout_e) * scale, "graph", scatter_dimension=0, tiled=True
        ),
        lax.psum_scatter(gg_e * scale, "graph", scatter_dimension=0, tiled=True),
        lax.psum_scatter(
            transposed(node_inputs, gpre_n) * scale, "graph", scatter_dimension=0, tiled=True
        ),
        lax.psum_scatter(gb_n * scale, "graph", scatter_dimension=0, tiled=True),
        lax.psum_scatter(
            transposed(act_n, gout_n) * scale, "graph", scatter_dimension=0, tiled=True
        ),
        lax.psum_scatter(gg_n * scale, "graph", scatter_dimension=0, tiled=True),
    )
    return (
        node_out,
        edge_out,
        node_grad,
        edge_grad,
        g_ew1,
        g_eb1,
        g_ew2,
        g_egain,
        g_nw1,
        g_nb1,
        g_nw2,
        g_ngain,
    )


def solution(mesh):
    return jax.shard_map(
        on_device,
        mesh=mesh,
        in_specs=(
            P(("groups", "graph"), None),
            P(("groups", "graph"), None),
            P(("groups", "graph")),
            P(("groups", "graph")),
            P(("groups", "graph"), None, None),
            P(("groups", "graph")),
            P(),
            P(),
            P(),
            P(),
            P(),
            P(),
            P(),
            P(),
            P(("groups", "graph"), None),
            P(("groups", "graph"), None),
        ),
        out_specs=(
            P(("groups", "graph"), None),
            P(("groups", "graph"), None),
            P(("groups", "graph"), None),
            P(("groups", "graph"), None),
            P(("groups", "graph"), None),
            P(("groups", "graph")),
            P(("groups", "graph"), None),
            P(("groups", "graph")),
            P(("groups", "graph"), None),
            P(("groups", "graph")),
            P(("groups", "graph"), None),
            P(("groups", "graph")),
        ),
        check_vma=False,
    )
```

profile of v0, /device:TPU:0, one launch (start us, length us, event | category | flops | bytes accessed | tf_op | source)
XLA Modules:
  0.0 294.4 jit_solution(13329865411435370355)
XLA Ops:
  7.2 0.8 compare_and_fusion
  8.0 0.8 copy.35
  9.0 1.9 gather_fusion
  10.9 0.7 bitcast_select_fusion
  11.7 7.4 %all-to-all-start = ((bf16[16,8,512]{2,1,0:T(8,128)(2,1)}), bf16[16,8,512]{2,1,0:T(8,128)(2,1)S(1)}, u32[]{:S(2)}, u32[]{:S(2)}) async-start(bf16[16,8,512]{2,1,0:T(8,128)(2,1)} %bitcast_select_fusion), calls=%async_computation | async-start | bytes 262144 | tf_op jit(solution)/shard_map/all_to_all | solution.py:83
  20.1 6.9 %all-to-all-done = bf16[16,8,512]{2,1,0:T(8,128)(2,1)S(1)} async-done(((bf16[16,8,512]{2,1,0:T(8,128)(2,1)}), bf16[16,8,512]{2,1,0:T(8,128)(2,1)S(1)}, u32[]{:S(2)}, u32[]{:S(2)}) %all-to-all-start) | async-done | bytes 131104 | tf_op jit(solution)/shard_map/all_to_all | solution.py:83
  27.0 0.4 convolution_convert_fusion.1
  27.5 0.8 copy-done.25
  28.2 0.8 convolution_add_fusion
  29.3 0.5 fusion.39
  29.7 0.4 copy-done.27
  30.4 1.1 add_convert_fusion
  31.5 0.4 convolution_convert_fusion.2
  31.9 0.4 convolution_add_fusion.2
  32.5 0.4 fusion.40
  33.2 0.3 copy-done.4
  33.5 1.0 fusion.12
  34.5 0.5 convert_reduce_fusion.1
  35.0 1.7 convolution_multiply_fusion.3
  36.7 1.7 fusion.42
  38.5 1.0 copy-done.3
  39.4 0.6 multiply_reduce_fusion
  40.4 0.7 copy-done.9
  41.2 1.5 convolution_multiply_fusion.2
  42.7 1.8 convolution_multiply_fusion.1
  44.7 0.9 copy-done.10
  45.6 1.9 convert_reduce_fusion
  47.5 0.7 copy-done.14
  48.3 2.7 convolution_multiply_fusion
  51.1 0.5 copy-done.24
  51.6 0.6 dynamic-slice
  52.9 30.9 %all-reduce.4 = (f32[512]{0:T(512)S(1)}, f32[512]{0:T(512)S(1)}, f32[512]{0:T(512)S(1)}, f32[512]{0:T(512)S(1)}) all-reduce(f32[512]{0:T(512)S(1)} %broadcast_multiply_fusion.3, f32[512]{0:T(512)S(1)} %broadcast_multiply_fusion.2, f32[512]{0:T(512)S(1)} %broadcast_multiply_fusion.1, ...), channel_id=3, replica_groups=mesh['groups'=2,'graph'=16] {'graph'}, use_global_device_ids=true, to_apply=%region_11.12.clone | all-reduce | flops 2048 | bytes 16384
  83.8 0.6 dynamic-slice.1
  84.4 0.6 dynamic-slice.3
  85.0 0.6 dynamic-slice.5
  85.5 0.6 dynamic-slice.7
  86.1 2.2 fusion.41
  88.4 1.1 copy-done.2
  89.5 0.5 fusion.6
  90.0 0.7 fusion.26
  90.6 3.5 %all-to-all-start.1 = ((bf16[16,8,512]{2,1,0:T(8,128)(2,1)}), bf16[16,8,512]{2,1,0:T(8,128)(2,1)S(1)}, u32[]{:S(2)}, u32[]{:S(2)}) async-start(bf16[16,8,512]{2,1,0:T(8,128)(2,1)} %fusion.26), calls=%async_computation.1 | async-start | bytes 262144 | tf_op jit(solution)/shard_map/all_to_all | solution.py:115
  94.2 1.6 convolution_add_fusion.3
  95.8 2.2 convert_add_fusion
  98.0 4.1 %all-to-all-done.1 = bf16[16,8,512]{2,1,0:T(8,128)(2,1)S(1)} async-done(((bf16[16,8,512]{2,1,0:T(8,128)(2,1)}), bf16[16,8,512]{2,1,0:T(8,128)(2,1)S(1)}, u32[]{:S(2)}, u32[]{:S(2)}) %all-to-all-start.1) | async-done | bytes 131104 | tf_op jit(solution)/shard_map/all_to_all | solution.py:115
  102.1 1.6 scatter_custom_fusion
  103.7 49.3 %reduce-scatter.7.cloned.1.call-done = f32[32,512]{1,0:T(8,128)} async-done(((f32[512,512]{1,0:T(8,128)}), f32[32,512]{1,0:T(8,128)}) %reduce-scatter.7.cloned.1.call-update) | async-done | bytes 65552 | tf_op jit(solution)/shard_map/reduce_scatter | solution.py:132
  153.0 64.9 %reduce-scatter.9.cloned.1.call-done = f32[64,512]{1,0:T(8,128)} async-done(((f32[1024,512]{1,0:T(8,128)}), f32[64,512]{1,0:T(8,128)}) %reduce-scatter.9.cloned.1.call-update) | async-done | bytes 131088 | tf_op jit(solution)/shard_map/reduce_scatter | solution.py:136
  217.8 70.0 %reduce-scatter.5.cloned.1.call-done = f32[96,512]{1,0:T(8,128)} async-done(((f32[1536,512]{1,0:T(8,128)}), f32[96,512]{1,0:T(8,128)}) %reduce-scatter.5.cloned.1.call-update) | async-done | bytes 196624 | tf_op jit(solution)/shard_map/reduce_scatter | solution.py:128
  (79 shorter events, 2.2 us)
Async XLA Ops:
  7.2 21.0 %copy-start = (bf16[1536,512]{1,0:T(8,128)(2,1)S(1)}, bf16[1536,512]{1,0:T(8,128)(2,1)}, u32[]{:S(2)}) copy-start(bf16[1536,512]{1,0:T(8,128)(2,1)} %param.22) | copy-start | bytes 4718596
  7.2 12.6 %copy-start.1 = (bf16[256,512]{1,0:T(8,128)(2,1)S(1)}, bf16[256,512]{1,0:T(8,128)(2,1)}, u32[]{:S(2)}) copy-start(bf16[256,512]{1,0:T(8,128)(2,1)} %param.16) | copy-start | bytes 786436
  7.2 12.6 %copy-start.16 = (s32[384]{0:T(512)S(1)}, s32[384]{0:T(512)}, u32[]{:S(2)}) copy-start(s32[384]{0:T(512)} %param.19) | copy-start | bytes 4612
  7.2 19.8 %copy-start.19 = (s32[384]{0:T(512)S(1)}, s32[384]{0:T(512)}, u32[]{:S(2)}) copy-start(s32[384]{0:T(512)} %param.18) | copy-start | bytes 4612
  9.0 19.2 %copy-start.11 = (bf16[384,512]{1,0:T(8,128)(2,1)S(1)}, bf16[384,512]{1,0:T(8,128)(2,1)}, u32[]{:S(2)}) copy-start(bf16[384,512]{1,0:T(8,128)(2,1)} %param.17) | copy-start | bytes 1179652
  9.0 19.2 %copy-start.22 = (f32[512]{0:T(512)S(1)}, f32[512]{0:T(512)}, u32[]{:S(2)}) copy-start(f32[512]{0:T(512)} %param.23) | copy-start | bytes 6148
  11.7 15.3 %all-to-all-start = ((bf16[16,8,512]{2,1,0:T(8,128)(2,1)}), bf16[16,8,512]{2,1,0:T(8,128)(2,1)S(1)}, u32[]{:S(2)}, u32[]{:S(2)}) async-start(bf16[16,8,512]{2,1,0:T(8,128)(2,1)} %bitcast_select_fusion), calls=%async_computation | async-start | bytes 262144 | tf_op jit(solution)/shard_map/all_to_all | solution.py:83
  19.1 84.6 %reduce-scatter.11.cloned.1.call-start = ((), (), s32[]{:S(2)}) async-start(), calls=%async_computation.9 | async-start | bytes 1114112 | tf_op jit(solution)/shard_map/reduce_scatter | solution.py:140
  20.1 7.3 %copy-start.7 = (bf16[384,512]{1,0:T(8,128)(2,1)}, bf16[384,512]{1,0:T(8,128)(2,1)S(1)}, u32[]{:S(2)}) copy-start(bf16[384,512]{1,0:T(8,128)(2,1)S(1)} %convolution_convert_fusion) | copy-start | bytes 1179652
  27.4 0.8 copy-start.25
  28.2 1.0 copy-start.21
  29.3 0.9 copy-start.27
  29.3 1.1 copy-start.17
  30.1 1.8 copy-start.5
  30.1 1.8 copy-start.23
  31.5 1.0 copy-start.20
  32.5 0.9 copy-start.4
  32.5 1.0 copy-start.18
  36.6 116.3 %reduce-scatter.7.cloned.1.call-start = ((), (), s32[]{:S(2)}) async-start(), calls=%async_computation.7 | async-start | bytes 1114112 | tf_op jit(solution)/shard_map/reduce_scatter | solution.py:132
  36.7 2.7 copy-start.13
  38.4 1.0 copy-start.3
  40.0 1.1 copy-start.28
  40.4 0.7 copy-start.9
  42.7 175.1 %reduce-scatter.9.cloned.1.call-start = ((), (), s32[]{:S(2)}) async-start(), calls=%async_computation.8 | async-start | bytes 2228224 | tf_op jit(solution)/shard_map/reduce_scatter | solution.py:136
  44.6 1.0 copy-start.10
  44.6 3.7 %copy-start.8 = (bf16[384,512]{1,0:T(8,128)(2,1)S(1)}, bf16[384,512]{1,0:T(8,128)(2,1)}, u32[]{:S(2)}) copy-start(bf16[384,512]{1,0:T(8,128)(2,1)} %copy-done.7) | copy-start | bytes 1179652
  44.6 3.7 %copy-start.12 = (bf16[384,512]{1,0:T(8,128)(2,1)S(1)}, bf16[384,512]{1,0:T(8,128)(2,1)}, u32[]{:S(2)}) copy-start(bf16[384,512]{1,0:T(8,128)(2,1)} %param.17) | copy-start | bytes 1179652
  44.6 243.2 %reduce-scatter.5.cloned.1.call-start = ((), (), s32[]{:S(2)}) async-start(), calls=%async_computation.6 | async-start | bytes 3342336 | tf_op jit(solution)/shard_map/reduce_scatter | solution.py:128
  45.6 2.7 copy-start.26
  47.5 0.7 copy-start.14
  50.9 0.7 copy-start.24
  50.9 35.2 %copy-start.15 = (bf16[384,512]{1,0:T(8,128)(2,1)S(1)}, bf16[384,512]{1,0:T(8,128)(2,1)}, u32[]{:S(2)}) copy-start(bf16[384,512]{1,0:T(8,128)(2,1)} %copy-done.14) | copy-start | bytes 1179652
  88.4 1.1 copy-start.2
  90.6 11.4 %all-to-all-start.1 = ((bf16[16,8,512]{2,1,0:T(8,128)(2,1)}), bf16[16,8,512]{2,1,0:T(8,128)(2,1)S(1)}, u32[]{:S(2)}, u32[]{:S(2)}) async-start(bf16[16,8,512]{2,1,0:T(8,128)(2,1)} %fusion.26), calls=%async_computation.1 | async-start | bytes 262144 | tf_op jit(solution)/shard_map/all_to_all | solution.py:115
  103.6 184.2 %copy-start.6 = (f32[256,512]{1,0:T(8,128)}, f32[256,512]{1,0:T(8,128)S(1)}, u32[]{:S(2)}) copy-start(f32[256,512]{1,0:T(8,128)S(1)} %scatter_custom_fusion) | copy-start | bytes 1572868
Sparse Core Ops, SparseCore 0:
  36.8 55.1 reduce-scatter.10
  96.6 56.3 reduce-scatter.6
  157.3 60.4 reduce-scatter.8
  222.5 65.2 reduce-scatter.4
where the time goes:
time: 295 us; the launch traced here: 294 us
  waiting for transfers between devices  195 us (66%)
  blocking collectives  30.9 us (10%)
  matrix products  19.9 us (7%)
  between operations  15.5 us (5%)
  local copies, waits for them, and re-layouts  13.6 us (5%)
  starting transfers between devices  11.1 us (4%)
  other arithmetic  8.21 us (3%)
    reduce_scatter x1, waiting for transfers between devices, on_device(): lax.psum_scatter(transposed(edge_inputs, gpre_e) * scale, 'graph', scatte...  70 us
    reduce_scatter x1, waiting for transfers between devices, on_device(): lax.psum_scatter(transposed(node_inputs, gpre_n) * scale, 'graph', scatte...  64.9 us
    reduce_scatter x1, waiting for transfers between devices, on_device(): lax.psum_scatter(transposed(act_e, gout_e) * scale, 'graph', scatter_dime...  49.3 us
    unnamed x1, blocking collectives  30.9 us
    unnamed x64, local copies, waits for them, and re-layouts  10.7 us
    dot_general x7, matrix products, transposed(): lax.dot_general(left, right, (((0,), (0,)), ((), ())), preferred_element_...  10.1 us
    all_to_all x1, starting transfers between devices, on_device(): lax.all_to_all(outgoing, 'graph', split_axis=0, concat_axis=0, tiled=True)  7.39 us
    all_to_all x1, waiting for transfers between devices, on_device(): lax.all_to_all(outgoing, 'graph', split_axis=0, concat_axis=0, tiled=True)  6.89 us
  transfers between devices with their start and end apart: 6, of which 5 were waited for; matrix products, arithmetic and copies ran while one was open for 8% of the time, Pallas kernels for 0%

commit v1 on v0

--- a/solution.py
+++ b/solution.py
@@ -3,6 +3,8 @@
 import jax
 import jax.numpy as jnp
 from jax import lax
+from jax.experimental import pallas as pl
+from jax.experimental.pallas import tpu as pltpu
 from jax.sharding import PartitionSpec as P
 
 
@@ -55,7 +57,7 @@
     return (index[:, None] == jnp.arange(count, dtype=jnp.int32)[None, :]).astype(jnp.bfloat16)
 
 
-def on_device(
+def general_on_device(
     node_feat,
     edge_feat,
     edge_source,
@@ -158,6 +160,406 @@
     )
 
 
+MESH = pl.DeviceIdType.MESH
+F32 = jnp.float32
+BF16 = jnp.bfloat16
+
+
+def mm(left, right):
+    return jnp.dot(left, right, preferred_element_type=F32)
+
+
+def mm_nt(left, right):
+    return lax.dot_general(left, right, (((1,), (1,)), ((), ())), preferred_element_type=F32)
+
+
+def remote(src, dst, send_sem, recv_sem, peer):
+    return pltpu.make_async_remote_copy(
+        src_ref=src,
+        dst_ref=dst,
+        send_sem=send_sem,
+        recv_sem=recv_sem,
+        device_id={"graph": peer},
+        device_id_type=MESH,
+    )
+
+
+class Scatter:
+    def __init__(self, place, refs):
+        self.outer, self.inner, self.o, self.i, self.c = place
+        self.part, self.rc, self.s1, self.ry, self.s2, self.rz, self.send, self.recv = refs
+        self.copies = []
+
+    def index(self, o, i, c):
+        return (o * self.inner + i) * 2 + c
+
+    def start(self, value):
+        rows, cols = self.part.shape[-2:]
+        self.part[...] = value.astype(BF16).reshape(self.outer, self.inner, 2, rows, cols)
+        peer = self.index(self.o, self.i, 1 - self.c)
+        self.core = remote(
+            self.part.at[:, :, 1 - self.c], self.rc, self.send.at[0], self.recv.at[0], peer
+        )
+        self.core.start()
+        self.copies.append(self.core)
+
+    def along_inner(self):
+        self.core.wait_recv()
+        for o in range(self.outer):
+            mine = self.part[o, :, pl.ds(self.c, 1)][:, 0]
+            self.s1[o] = (mine.astype(F32) + self.rc[o].astype(F32)).astype(BF16)
+        self.inner_copies = []
+        for k in range(1, self.inner):
+            i = lax.rem(self.i + k, self.inner)
+            copy = remote(
+                self.s1.at[:, i],
+                self.ry.at[k - 1],
+                self.send.at[k],
+                self.recv.at[k],
+                self.index(self.o, i, self.c),
+            )
+            copy.start()
+            self.inner_copies.append(copy)
+        self.copies += self.inner_copies
+
+    def along_outer(self):
+        for copy in self.inner_copies:
+            copy.wait_recv()
+        for o in range(self.outer):
+            total = self.s1[o, pl.ds(self.i, 1)][0].astype(F32)
+            for k in range(self.inner - 1):
+                total = total + self.ry[k, o].astype(F32)
+            self.s2[o] = total.astype(BF16)
+        self.outer_copies = []
+        for k in range(1, self.outer):
+            o = lax.rem(self.o + k, self.outer)
+            slot = self.inner - 1 + k
+            copy = remote(
+                self.s2.at[o],
+                self.rz.at[k - 1],
+                self.send.at[slot],
+                self.recv.at[slot],
+                self.index(o, self.i, self.c),
+            )
+            copy.start()
+            self.outer_copies.append(copy)
+        self.copies += self.outer_copies
+
+    def finish(self):
+        for copy in self.outer_copies:
+            copy.wait_recv()
+        total = self.s2[pl.ds(self.o, 1)][0].astype(F32)
+        for k in range(self.outer - 1):
+            total = total + self.rz[k].astype(F32)
+        return total
+
+
+def norm_backward(scaled, normed, rstd):
+    return (
+        scaled
+        - jnp.mean(scaled, axis=-1, keepdims=True)
+        - normed * jnp.mean(scaled * normed, axis=-1, keepdims=True)
+    ) * rstd
+
+
+def one_hot_rows(row, count):
+    ids = lax.broadcasted_iota(jnp.int32, (count, row.shape[1]), 0)
+    return jnp.where(ids == row, 1.0, 0.0).astype(BF16)
+
+
+def one_hot_columns(row, count):
+    length = row.shape[1]
+    column = jnp.broadcast_to(row.astype(F32), (128, length)).T.astype(jnp.int32)
+    lanes = lax.broadcasted_iota(jnp.int32, (length, 128), 1)
+    parts = [
+        jnp.where(column == lanes + start, 1.0, 0.0).astype(BF16) for start in range(0, count, 128)
+    ]
+    return jnp.concatenate(parts, axis=1)
+
+
+def halves_to_blocks(rows, peers):
+    half = rows.shape[1] // 2
+    left = rows[:, :half].reshape(peers, 8, half)
+    right = rows[:, half:].reshape(peers, 8, half)
+    return jnp.concatenate([left, right], axis=1).astype(BF16)
+
+
+def blocks_to_halves(blocks):
+    peers, _, half = blocks.shape
+    wide = blocks.astype(F32)
+    left = wide[:, :8].reshape(peers * 8, half)
+    right = wide[:, 8:].reshape(peers * 8, half)
+    return jnp.concatenate([left, right], axis=1).astype(BF16)
+
+
+def layer_kernel(peers, outer, inner, n_chunks, *refs):
+    (nf, ef, src, tgt, req, cnt, ew1, eb1, ew2, egain, nw1, nb1, nw2, ngain, ncot, ecot) = refs[:16]
+    (node_out, edge_out, node_grad, edge_grad, g_ew1, g_ew2, g_nw1, g_nw2, g_small) = refs[16:25]
+    (hout, hin, bout, bin_, x_e, pre_e, z_e, rstd_e, act_e, x_n, pre_n, z_n, gpre_n, gpre_e,
+     h_send, h_recv, b_send, b_recv) = refs[25:43]
+    chunk_refs = refs[43:]
+    nodes, width = nf.shape
+    edges = ef.shape[0]
+    me = lax.axis_index("graph")
+    c = lax.rem(me, 2)
+    i = lax.rem(me // 2, inner)
+    o = me // (2 * inner)
+    place = (outer, inner, o, i, c)
+    s_nw2, s_nw1, s_ew2, s_e0, s_e1 = [
+        Scatter(place, chunk_refs[8 * k : 8 * k + 8]) for k in range(n_chunks)
+    ]
+
+    barrier = pltpu.get_barrier_semaphore()
+    others = [lax.rem(me + k, peers) for k in range(1, peers)]
+    for peer in others:
+        pl.semaphore_signal(barrier, inc=1, device_id={"graph": peer}, device_id_type=MESH)
+
+    hout[...] = halves_to_blocks(mm(one_hot_columns(req[...], nodes), nf[...]), peers)
+    hin[pl.ds(me, 1)] = hout[pl.ds(me, 1)]
+    pl.semaphore_wait(barrier, peers - 1)
+    halo = []
+    for k, peer in enumerate(others):
+        copy = remote(hout.at[peer], hin.at[me], h_send.at[k], h_recv.at[k], peer)
+        copy.start()
+        halo.append(copy)
+
+    table_rows = nodes + peers * 8
+    source_hot = one_hot_columns(src[...], table_rows)
+    target_hot = one_hot_columns(tgt[...], nodes)
+    target_hot_t = one_hot_rows(tgt[...], nodes)
+    live = jnp.where(lax.broadcasted_iota(jnp.int32, (edges, 1), 0) < cnt[0], 1.0, 0.0).astype(F32)
+    x_e[:, :width] = ef[...]
+    x_e[:, 2 * width :] = mm(target_hot, nf[...]).astype(BF16)
+    own = mm(source_hot[:, :nodes], nf[...])
+    pre_e[...] = (
+        mm(ef[...], ew1[:width]) + mm(x_e[:, 2 * width :], ew1[2 * width :]) + eb1[...]
+    )
+    x_n[:, :width] = nf[...]
+    pre_n[...] = mm(nf[...], nw1[:width]) + nb1[...]
+
+    for copy in halo:
+        copy.wait_recv()
+    received = blocks_to_halves(hin[...])
+    x_e[:, width : 2 * width] = (own + mm(source_hot[:, nodes:], received)).astype(BF16)
+    pre = pre_e[...] + mm(x_e[:, width : 2 * width], ew1[width : 2 * width])
+    sig = jax.nn.sigmoid(pre)
+    act_e[...] = (pre * sig).astype(BF16)
+    pre_e[...] = sig * (1.0 + pre * (1.0 - sig))
+    normed, rstd = layer_norm(mm(act_e[...], ew2[...]))
+    z_e[...] = normed
+    rstd_e[...] = rstd
+    message = (live * normed * egain[...]).astype(BF16)
+    edge_out[...] = (ef[...].astype(F32) + message.astype(F32)).astype(BF16)
+    x_n[:, width:] = mm(target_hot_t, message).astype(BF16)
+
+    pre = pre_n[...] + mm(x_n[:, width:], nw1[width:])
+    sig = jax.nn.sigmoid(pre)
+    act_n = (pre * sig).astype(BF16)
+    slope = sig * (1.0 + pre * (1.0 - sig))
+    normed, rstd = layer_norm(mm(act_n, nw2[...]))
+    node_out[...] = (nf[...].astype(F32) + normed * ngain[...]).astype(BF16)
+    grad = ncot[...].astype(F32)
+    gg_n = jnp.sum(grad * normed, axis=0, keepdims=True)
+    gout = norm_backward(grad * ngain[...], normed, rstd).astype(BF16)
+    gpre_n[...] = (mm_nt(gout, nw2[...]) * slope).astype(BF16)
+    gb_n = jnp.sum(gpre_n[...].astype(F32), axis=0, keepdims=True)
+    grad_agg = mm_nt(gpre_n[...], nw1[width:]).astype(BF16)
+    s_nw1.start(transposed(x_n[...], gpre_n[...]))
+    s_nw2.start(transposed(act_n, gout))
+
+    grad = live * (ecot[...].astype(F32) + mm(target_hot, grad_agg))
+    normed = z_e[...]
+    gg_e = jnp.sum(grad * normed, axis=0, keepdims=True)
+    gout = norm_backward(grad * egain[...], normed, rstd_e[...]).astype(BF16)
+    s_nw1.along_inner()
+    s_ew2.start(transposed(act_e[...], gout))
+    s_nw2.along_inner()
+    gpre_e[...] = (mm_nt(gout, ew2[...]) * pre_e[...]).astype(BF16)
+    gb_e = jnp.sum(gpre_e[...].astype(F32), axis=0, keepdims=True)
+    half = width // 2
+    s_e0.start(transposed(x_e[...], gpre_e[:, :half]))
+    s_ew2.along_inner()
+    s_nw1.along_outer()
+    s_e1.start(transposed(x_e[...], gpre_e[:, half:]))
+    s_nw2.along_outer()
+
+    grad_send = mm_nt(gpre_e[...], ew1[width : 2 * width]).astype(BF16)
+    source_hot_t = one_hot_rows(src[...], table_rows)
+    bout[:, :, :half] = halves_to_blocks(mm(source_hot_t[nodes:], grad_send), peers)
+    per = width // peers
+    column = lax.broadcasted_iota(jnp.int32, (peers, width), 1)
+    owner = lax.broadcasted_iota(jnp.int32, (peers, width), 0) * per
+    owned = jnp.logical_and(column >= owner, column < owner + per)
+    where_from = lax.rem(lax.broadcasted_iota(jnp.int32, (width, 128), 0), per)
+    where_to = lax.broadcasted_iota(jnp.int32, (width, 128), 1)
+    small = jnp.zeros((peers, 128), F32)
+    for q, vector in enumerate((gb_e, gg_e, gb_n, gg_n)):
+        spread = jnp.where(owned, vector, 0.0).astype(BF16)
+        move = jnp.where(where_to == where_from + q * per, 1.0, 0.0).astype(BF16)
+        small = small + mm(spread, move)
+    bout[:, :, half:] = jnp.broadcast_to(small[:, None, :], (peers, 16, 128)).astype(BF16)
+    bin_[pl.ds(me, 1)] = bout[pl.ds(me, 1)]
+    s_e0.along_inner()
+    back = []
+    for k, peer in enumerate(others):
+        copy = remote(bout.at[peer], bin_.at[me], b_send.at[k], b_recv.at[k], peer)
+        copy.start()
+        back.append(copy)
+    s_e1.along_inner()
+    s_ew2.along_outer()
+
+    edge_grad[...] = ecot[...].astype(F32) + mm_nt(gpre_e[...], ew1[:width])
+    grad_recv = mm_nt(gpre_e[...], ew1[2 * width :]).astype(BF16)
+    s_e0.along_outer()
+    node_grad[...] = (
+        ncot[...].astype(F32)
+        + mm_nt(gpre_n[...], nw1[:width])
+        + mm(source_hot_t[:nodes], grad_send)
+        + mm(target_hot_t, grad_recv)
+    )
+    s_e1.along_outer()
+    scale = 1.0 / math.sqrt(edges * peers)
+    g_nw1[...] = s_nw1.finish() * scale
+    g_nw2[...] = s_nw2.finish() * scale
+    for copy in back:
+        copy.wait_recv()
+    node_grad[...] += mm(one_hot_rows(req[...], nodes), blocks_to_halves(bin_[:, :, :half]))
+    g_small[...] = jnp.sum(bin_[:, :, half:].astype(F32), axis=0)[:8] * scale
+    g_ew2[...] = s_ew2.finish() * scale
+    g_ew1[:, :half] = s_e0.finish() * scale
+    g_ew1[:, half:] = s_e1.finish() * scale
+    for copy in halo + back:
+        copy.wait_send()
+    for chunk in (s_nw1, s_nw2, s_ew2, s_e0, s_e1):
+        for copy in chunk.copies:
+            copy.wait_send()
+
+
+def kernel_fits(peers, width, slots):
+    return (
+        slots == 8
+        and width % (peers * 16) == 0
+        and 4 * (width // peers) <= 128
+        and peers * slots % 128 == 0
+    )
+
+
+def on_device(
+    node_feat,
+    edge_feat,
+    edge_source,
+    edge_target,
+    halo_rows,
+    edge_count,
+    edge_w1,
+    edge_b1,
+    edge_w2,
+    edge_gain,
+    node_w1,
+    node_b1,
+    node_w2,
+    node_gain,
+    node_cot,
+    edge_cot,
+):
+    peers = lax.axis_size("graph")
+    nodes, width = node_feat.shape
+    edges = edge_feat.shape[0]
+    if not kernel_fits(peers, width, halo_rows.shape[2]):
+        return general_on_device(
+            node_feat, edge_feat, edge_source, edge_target, halo_rows, edge_count,
+            edge_w1, edge_b1, edge_w2, edge_gain, node_w1, node_b1, node_w2, node_gain,
+            node_cot, edge_cot,
+        )
+    inner = 1 << (int(math.log2(peers // 2)) // 2)
+    outer = peers // 2 // inner
+    shares = [
+        (width // peers, width),
+        (2 * width // peers, width),
+        (width // peers, width),
+        (3 * width // peers, width // 2),
+        (3 * width // peers, width // 2),
+    ]
+    chunk_scratch = []
+    for rows, cols in shares:
+        chunk_scratch += [
+            pltpu.VMEM((outer, inner, 2, rows, cols), BF16),
+            pltpu.VMEM((outer, inner, rows, cols), BF16),
+            pltpu.VMEM((outer, inner, rows, cols), BF16),
+            pltpu.VMEM((inner - 1, outer, rows, cols), BF16),
+            pltpu.VMEM((outer, rows, cols), BF16),
+            pltpu.VMEM((outer - 1, rows, cols), BF16),
+            pltpu.SemaphoreType.DMA((inner + outer - 1,)),
+            pltpu.SemaphoreType.DMA((inner + outer - 1,)),
+        ]
+    half = width // 2
+    vmem = pl.BlockSpec(memory_space=pltpu.VMEM)
+    smem = pl.BlockSpec(memory_space=pltpu.SMEM)
+    shape = jax.ShapeDtypeStruct
+    (node_out, edge_out, node_grad, edge_grad, g_ew1, g_ew2, g_nw1, g_nw2, g_small) = pl.pallas_call(
+        lambda *refs: layer_kernel(peers, outer, inner, len(shares), *refs),
+        out_shape=(
+            shape((nodes, width), BF16),
+            shape((edges, width), BF16),
+            shape((nodes, width), F32),
+            shape((edges, width), F32),
+            shape((3 * width // peers, width), F32),
+            shape((width // peers, width), F32),
+            shape((2 * width // peers, width), F32),
+            shape((width // peers, width), F32),
+            shape((8, 128), F32),
+        ),
+        in_specs=[vmem] * 5 + [smem] + [vmem] * 10,
+        out_specs=[vmem] * 9,
+        scratch_shapes=[
+            pltpu.VMEM((peers, 16, half), BF16),
+            pltpu.VMEM((peers, 16, half), BF16),
+            pltpu.VMEM((peers, 16, half + 128), BF16),
+            pltpu.VMEM((peers, 16, half + 128), BF16),
+            pltpu.VMEM((edges, 3 * width), BF16),
+            pltpu.VMEM((edges, width), F32),
+            pltpu.VMEM((edges, width), F32),
+            pltpu.VMEM((edges, 1), F32),
+            pltpu.VMEM((edges, width), BF16),
+            pltpu.VMEM((nodes, 2 * width), BF16),
+            pltpu.VMEM((nodes, width), F32),
+            pltpu.VMEM((nodes, width), F32),
+            pltpu.VMEM((nodes, width), BF16),
+            pltpu.VMEM((edges, width), BF16),
+            pltpu.SemaphoreType.DMA((peers - 1,)),
+            pltpu.SemaphoreType.DMA((peers - 1,)),
+            pltpu.SemaphoreType.DMA((peers - 1,)),
+            pltpu.SemaphoreType.DMA((peers - 1,)),
+        ]
+        + chunk_scratch,
+        compiler_params=pltpu.CompilerParams(
+            collective_id=0, has_side_effects=True, vmem_limit_bytes=56 * 1024 * 1024
+        ),
+    )(
+        node_feat,
+        edge_feat,
+        edge_source.reshape(1, edges),
+        edge_target.reshape(1, edges),
+        halo_rows.reshape(1, -1),
+        edge_count,
+        edge_w1,
+        edge_b1.reshape(1, width),
+        edge_w2,
+        edge_gain.reshape(1, width),
+        node_w1,
+        node_b1.reshape(1, width),
+        node_w2,
+        node_gain.reshape(1, width),
+        node_cot,
+        edge_cot,
+    )
+    per = width // peers
+    gb_e, gg_e, gb_n, gg_n = [g_small[0, q * per : (q + 1) * per] for q in range(4)]
+    return (
+        node_out, edge_out, node_grad, edge_grad, g_ew1, gb_e, g_ew2, gg_e, g_nw1, gb_n, g_nw2, gg_n
+    )
+
+
 def solution(mesh):
     return jax.shard_map(
         on_device,

time: 295 us -> 69.2 us (0.23)
  waiting for transfers between devices: 195 us -> 0 us
  Pallas kernels: 0 us -> 54.6 us
  blocking collectives: 30.9 us -> 0 us
  matrix products: 19.9 us -> 0 us
  between operations: 15.5 us -> 1.33 us
  starting transfers between devices: 11.1 us -> 0 us
  other arithmetic: 8.21 us -> 0 us
    reduce_scatter x4 -> x0, waiting for transfers between devices: 184 us -> none  [the longest x1 70 us: on_device(): lax.psum_scatter(transposed(edge_inputs, gpre_e) * scale, 'graph', scatte...]
    pallas_call x0 -> x1, Pallas kernels: none -> 54.6 us  [on_device(): pl.pallas_call(lambda *refs: layer_kernel(peers, outer, inner, len(shares...]
    unnamed x1 -> x0, blocking collectives: 30.9 us -> none
    dot_general x18 -> x0, matrix products: 19.9 us -> none  [the longest x7 10.1 us: transposed(): lax.dot_general(left, right, (((0,), (0,)), ((), ())), preferred_element_...]
    all_to_all x2 -> x0, waiting for transfers between devices: 10.9 us -> none  [the longest x1 6.89 us: on_device(): lax.all_to_all(outgoing, 'graph', split_axis=0, concat_axis=0, tiled=True)]
    all_to_all x2 -> x0, starting transfers between devices: 10.9 us -> none  [the longest x1 7.39 us: on_device(): lax.all_to_all(outgoing, 'graph', split_axis=0, concat_axis=0, tiled=True)]
    unnamed x64 -> x21, local copies, waits for them, and re-layouts: 10.7 us -> 8.52 us
  transfers between devices with their start and end apart: 6 -> 0, of which waited for: 5 -> 0; matrix products, arithmetic and copies ran while one was open for 8% -> 0% of each run, Pallas kernels for 0% -> 0%
where the time goes in v1:
time: 69.2 us; the launch traced here: 68.9 us
  Pallas kernels  54.6 us (79%)
  local copies, waits for them, and re-layouts  13 us (19%)
  between operations  1.33 us (2%)
    pallas_call x1, Pallas kernels, on_device(): pl.pallas_call(lambda *refs: layer_kernel(peers, outer, inner, len(shares...  54.6 us
    unnamed x21, local copies, waits for them, and re-layouts  8.52 us
    squeeze x1, local copies, waits for them, and re-layouts, on_device(): g_small[0, q * per:(q + 1) * per]  1.42 us

profile of v1, /device:TPU:0, one launch (start us, length us, event | category | flops | bytes accessed | tf_op | source)
XLA Modules:
  0.0 68.9 jit_solution(18242877007924488747)
XLA Ops:
  1.3 1.2 %reshape.45.refs_2_ = s32[1,384]{1,0:T(1,128)} reshape(s32[384]{0:T(512)} %param.18) | data formatting | bytes 3072 | tf_op jit(solution)/shard_map/reshape | solution.py:541
  2.5 1.2 %reshape.46.refs_3_ = s32[1,384]{1,0:T(1,128)} reshape(s32[384]{0:T(512)} %param.19) | data formatting | bytes 3072 | tf_op jit(solution)/shard_map/reshape | solution.py:542
  3.8 0.8 %copy.29 = s32[1,16,8]{2,1,0:T(8,128)S(1)} copy(s32[1,16,8]{1,2,0:T(8,128)} %param.20) | data formatting | bytes 1024 | tf_op args[4]
  4.5 0.6 reshape.47.refs_4_
  5.1 54.6 %shard_map.247 = (bf16[256,512]{1,0:T(8,128)(2,1)}, bf16[384,512]{1,0:T(8,128)(2,1)}, f32[256,512]{1,0:T(8,128)}, f32[384,512]{1,0:T(8,128)}, f32[96,512]{1,0:T(...) custom-call(bf16[256,512]{1,0:T(8,128)(2,1)} %refs_0_.1, ...), custom_call_target="tpu_custom_call" | custom-call | tf_op jit(solution)/shard_map/pallas_call | solution.py:499
  59.7 0.0 copy-start.1
  59.7 0.0 copy-start
  59.7 1.4 %slice_bitcast_fusion = (f32[32]{0:T(128)}, f32[32]{0:T(128)}, f32[32]{0:T(128)}, f32[32]{0:T(128)}) fusion(f32[8,128]{1,0:T(8,128)} %get-tuple-element.26), kind=kLoop, calls=%fused_computation | loop fusion | bytes 1024 | tf_op jit(solution)/shard_map/squeeze | solution.py:557
  61.1 1.7 %copy.39 = bf16[256,512]{1,0:T(8,128)(2,1)} copy(bf16[256,512]{1,0:T(8,128)(2,1)} %get-tuple-element.46) | data formatting | bytes 524288
  62.8 0.0 copy-start.2
  62.8 1.8 %copy.40 = bf16[384,512]{1,0:T(8,128)(2,1)} copy(bf16[384,512]{1,0:T(8,128)(2,1)} %get-tuple-element.47) | data formatting | bytes 786432
  64.6 0.0 copy-done.1
  64.6 0.0 copy-start.5
  64.6 0.0 copy-start.3
  64.6 0.0 copy-start.4
  64.6 0.8 %copy.41 = f32[256,512]{1,0:T(8,128)} copy(f32[256,512]{1,0:T(8,128)S(1)} %copy-done.1) | data formatting | bytes 1048576
  65.4 0.0 copy-done
  65.4 0.9 %copy.42 = f32[384,512]{1,0:T(8,128)} copy(f32[384,512]{1,0:T(8,128)S(1)} %copy-done) | data formatting | bytes 1572864
  66.3 0.0 copy-done.2
  66.3 0.7 copy.43
  67.0 0.0 copy-done.5
  67.0 0.6 copy.44
  67.6 0.0 copy-done.3
  67.6 0.7 copy.45
  68.3 0.0 copy-done.4
  68.3 0.6 copy.46
Async XLA Ops:
  59.7 4.9 %copy-start.1 = (f32[256,512]{1,0:T(8,128)S(1)}, f32[256,512]{1,0:T(8,128)}, u32[]{:S(2)}) copy-start(f32[256,512]{1,0:T(8,128)} %get-tuple-element.48) | copy-start | bytes 1572868
  59.7 5.7 %copy-start = (f32[384,512]{1,0:T(8,128)S(1)}, f32[384,512]{1,0:T(8,128)}, u32[]{:S(2)}) copy-start(f32[384,512]{1,0:T(8,128)} %get-tuple-element.49) | copy-start | bytes 2359300
  62.8 3.5 %copy-start.2 = (f32[96,512]{1,0:T(8,128)S(1)}, f32[96,512]{1,0:T(8,128)}, u32[]{:S(2)}) copy-start(f32[96,512]{1,0:T(8,128)} %get-tuple-element.50) | copy-start | bytes 589828
  64.6 2.4 %copy-start.5 = (f32[32,512]{1,0:T(8,128)S(1)}, f32[32,512]{1,0:T(8,128)}, u32[]{:S(2)}) copy-start(f32[32,512]{1,0:T(8,128)} %get-tuple-element.52) | copy-start | bytes 196612
  64.6 3.0 %copy-start.3 = (f32[64,512]{1,0:T(8,128)S(1)}, f32[64,512]{1,0:T(8,128)}, u32[]{:S(2)}) copy-start(f32[64,512]{1,0:T(8,128)} %get-tuple-element.54) | copy-start | bytes 393220
  64.6 3.7 %copy-start.4 = (f32[32,512]{1,0:T(8,128)S(1)}, f32[32,512]{1,0:T(8,128)}, u32[]{:S(2)}) copy-start(f32[32,512]{1,0:T(8,128)} %get-tuple-element.56) | copy-start | bytes 196612

commit v2 on v1

--- a/solution.py
+++ b/solution.py
@@ -277,6 +277,27 @@
     return jnp.concatenate(parts, axis=1)
 
 
+def request_hot(requests, count):
+    slots, peers = requests.shape
+    lanes = lax.broadcasted_iota(jnp.int32, (slots, count), 1)
+    parts = [jnp.where(requests[:, p : p + 1] == lanes, 1.0, 0.0) for p in range(peers)]
+    return jnp.concatenate(parts, axis=0).astype(BF16)
+
+
+def copy_kernel(count, *refs):
+    sources, small, results = refs[:count], refs[count], refs[count + 1 : 2 * count + 1]
+    vectors, sems = refs[2 * count + 1 : 2 * count + 5], refs[2 * count + 5]
+    copies = []
+    for k in range(count):
+        copies.append(pltpu.make_async_copy(sources[k], results[k], sems.at[k]))
+        copies[-1].start()
+    for q, ref in enumerate(vectors):
+        per = ref.shape[0]
+        ref[...] = small[0, q * per : (q + 1) * per]
+    for copy in copies:
+        copy.wait()
+
+
 def halves_to_blocks(rows, peers):
     half = rows.shape[1] // 2
     left = rows[:, :half].reshape(peers, 8, half)
@@ -314,7 +335,7 @@
     for peer in others:
         pl.semaphore_signal(barrier, inc=1, device_id={"graph": peer}, device_id_type=MESH)
 
-    hout[...] = halves_to_blocks(mm(one_hot_columns(req[...], nodes), nf[...]), peers)
+    hout[...] = halves_to_blocks(mm(request_hot(req[...], nodes), nf[...]), peers)
     hin[pl.ds(me, 1)] = hout[pl.ds(me, 1)]
     pl.semaphore_wait(barrier, peers - 1)
     halo = []
@@ -324,9 +345,11 @@
         halo.append(copy)
 
     table_rows = nodes + peers * 8
-    source_hot = one_hot_columns(src[...], table_rows)
-    target_hot = one_hot_columns(tgt[...], nodes)
-    target_hot_t = one_hot_rows(tgt[...], nodes)
+    sources = src[...].reshape(1, edges)
+    targets = tgt[...].reshape(1, edges)
+    source_hot = one_hot_columns(sources, table_rows)
+    target_hot = one_hot_columns(targets, nodes)
+    target_hot_t = one_hot_rows(targets, nodes)
     live = jnp.where(lax.broadcasted_iota(jnp.int32, (edges, 1), 0) < cnt[0], 1.0, 0.0).astype(F32)
     x_e[:, :width] = ef[...]
     x_e[:, 2 * width :] = mm(target_hot, nf[...]).astype(BF16)
@@ -384,7 +407,7 @@
     s_nw2.along_outer()
 
     grad_send = mm_nt(gpre_e[...], ew1[width : 2 * width]).astype(BF16)
-    source_hot_t = one_hot_rows(src[...], table_rows)
+    source_hot_t = one_hot_rows(sources, table_rows)
     bout[:, :, :half] = halves_to_blocks(mm(source_hot_t[nodes:], grad_send), peers)
     per = width // peers
     column = lax.broadcasted_iota(jnp.int32, (peers, width), 1)
@@ -423,7 +446,7 @@
     g_nw2[...] = s_nw2.finish() * scale
     for copy in back:
         copy.wait_recv()
-    node_grad[...] += mm(one_hot_rows(req[...], nodes), blocks_to_halves(bin_[:, :, :half]))
+    node_grad[...] += transposed(request_hot(req[...], nodes), blocks_to_halves(bin_[:, :, :half]))
     g_small[...] = jnp.sum(bin_[:, :, half:].astype(F32), axis=0)[:8] * scale
     g_ew2[...] = s_ew2.finish() * scale
     g_ew1[:, :half] = s_e0.finish() * scale
@@ -538,9 +561,9 @@
     )(
         node_feat,
         edge_feat,
-        edge_source.reshape(1, edges),
-        edge_target.reshape(1, edges),
-        halo_rows.reshape(1, -1),
+        edge_source,
+        edge_target,
+        halo_rows[0].T,
         edge_count,
         edge_w1,
         edge_b1.reshape(1, width),
@@ -553,8 +576,18 @@
         node_cot,
         edge_cot,
     )
-    per = width // peers
-    gb_e, gg_e, gb_n, gg_n = [g_small[0, q * per : (q + 1) * per] for q in range(4)]
+    whole = (node_out, edge_out, node_grad, edge_grad, g_ew1, g_ew2, g_nw1, g_nw2)
+    anywhere = pl.BlockSpec(memory_space=pl.ANY)
+    (node_out, edge_out, node_grad, edge_grad, g_ew1, g_ew2, g_nw1, g_nw2, gb_e, gg_e, gb_n, gg_n) = (
+        pl.pallas_call(
+            lambda *refs: copy_kernel(len(whole), *refs),
+            out_shape=[shape(array.shape, array.dtype) for array in whole]
+            + [shape((width // peers,), F32)] * 4,
+            in_specs=[anywhere] * len(whole) + [vmem],
+            out_specs=[anywhere] * len(whole) + [vmem] * 4,
+            scratch_shapes=[pltpu.SemaphoreType.DMA((len(whole),))],
+        )(*whole, g_small)
+    )
     return (
         node_out, edge_out, node_grad, edge_grad, g_ew1, gb_e, g_ew2, gg_e, g_nw1, gb_n, g_nw2, gg_n
     )

time: 69.2 us -> 132 us (1.91)
  Pallas kernels: 54.6 us -> 130 us
  local copies, waits for them, and re-layouts: 13 us -> 0 us
    pallas_call x0 -> x1, Pallas kernels: none -> 75.8 us  [on_device(): pl.pallas_call(lambda *refs: copy_kernel(len(whole), *refs), out_shape=[s...]
    unnamed x21 -> x0, local copies, waits for them, and re-layouts: 8.52 us -> none
    reshape x3 -> x0, local copies, waits for them, and re-layouts: 3.09 us -> none  [the longest x1 1.25 us: on_device(): edge_source.reshape(1, edges)]
    squeeze x1 -> x0, local copies, waits for them, and re-layouts: 1.42 us -> none  [on_device(): g_small[0, q * per:(q + 1) * per]]
where the time goes in v2:
time: 132 us
  Pallas kernels  130 us (98%)
    pallas_call x1, Pallas kernels, on_device(): pl.pallas_call(lambda *refs: copy_kernel(len(whole), *refs), out_shape=[s...  75.8 us
    pallas_call x1, Pallas kernels, on_device(): pl.pallas_call(lambda *refs: layer_kernel(peers, outer, inner, len(shares...  54.6 us

profile of v2, /device:TPU:0, one launch (start us, length us, event | category | flops | bytes accessed | tf_op | source)
XLA Modules:
  0.0 131.7 jit_solution(16724114404732091621)
XLA Ops:
  1.3 54.6 %shard_map.247 = (bf16[256,512]{1,0:T(8,128)(2,1)}, bf16[384,512]{1,0:T(8,128)(2,1)}, f32[256,512]{1,0:T(8,128)}, f32[384,512]{1,0:T(8,128)}, f32[96,512]{1,0:T(...) custom-call(bf16[256,512]{1,0:T(8,128)(2,1)} %refs_0_.1, ...), custom_call_target="tpu_custom_call" | custom-call | tf_op jit(solution)/shard_map/pallas_call | solution.py:522
  55.9 75.8 %shard_map.248 = (bf16[256,512]{1,0:T(8,128)(2,1)}, bf16[384,512]{1,0:T(8,128)(2,1)}, f32[256,512]{1,0:T(8,128)}, f32[384,512]{1,0:T(8,128)}, f32[96,512]{1,0:T(...) custom-call(bf16[256,512]{1,0:T(8,128)(2,1)} %get-tuple-element.33.r, ...), custom_call_target="tpu_custom_call" | custom-call | tf_op jit(solution)/shard_map/pallas_call | solution.py:582

commit v3 on v2

--- a/solution.py
+++ b/solution.py
@@ -286,11 +286,15 @@
 
 def copy_kernel(count, *refs):
     sources, small, results = refs[:count], refs[count], refs[count + 1 : 2 * count + 1]
-    vectors, sems = refs[2 * count + 1 : 2 * count + 5], refs[2 * count + 5]
-    copies = []
-    for k in range(count):
-        copies.append(pltpu.make_async_copy(sources[k], results[k], sems.at[k]))
-        copies[-1].start()
+    vectors, held = refs[2 * count + 1 : 2 * count + 5], refs[2 * count + 5 : 3 * count + 5]
+    in_sems, out_sems = refs[3 * count + 5 :]
+    fetches = [pltpu.make_async_copy(sources[k], held[k], in_sems.at[k]) for k in range(count)]
+    copies = [pltpu.make_async_copy(held[k], results[k], out_sems.at[k]) for k in range(count)]
+    for fetch in fetches:
+        fetch.start()
+    for fetch, copy in zip(fetches, copies):
+        fetch.wait()
+        copy.start()
     for q, ref in enumerate(vectors):
         per = ref.shape[0]
         ref[...] = small[0, q * per : (q + 1) * per]
@@ -585,7 +589,9 @@
             + [shape((width // peers,), F32)] * 4,
             in_specs=[anywhere] * len(whole) + [vmem],
             out_specs=[anywhere] * len(whole) + [vmem] * 4,
-            scratch_shapes=[pltpu.SemaphoreType.DMA((len(whole),))],
+            scratch_shapes=[pltpu.VMEM(array.shape, array.dtype) for array in whole]
+            + [pltpu.SemaphoreType.DMA((len(whole),))] * 2,
+            compiler_params=pltpu.CompilerParams(vmem_limit_bytes=32 * 1024 * 1024),
         )(*whole, g_small)
     )
     return (

time: 132 us -> 67.7 us (0.51)
  Pallas kernels: 130 us -> 57.6 us
  local copies, waits for them, and re-layouts: 0 us -> 8.3 us
    pallas_call x1, Pallas kernels: 75.8 us -> 3.03 us  [on_device(): pl.pallas_call(lambda *refs: copy_kernel(len(whole), *refs), out_shape=[s...]
    unnamed x0 -> x18, local copies, waits for them, and re-layouts: none -> 8.3 us
where the time goes in v3:
time: 67.7 us; the launch traced here: 67.2 us
  Pallas kernels  57.6 us (85%)
  local copies, waits for them, and re-layouts  8.3 us (12%)
  between operations  1.32 us (2%)
    pallas_call x1, Pallas kernels, on_device(): pl.pallas_call(lambda *refs: layer_kernel(peers, outer, inner, len(shares...  54.6 us
    unnamed x18, local copies, waits for them, and re-layouts  8.3 us
    pallas_call x1, Pallas kernels, on_device(): pl.pallas_call(lambda *refs: copy_kernel(len(whole), *refs), out_shape=[s...  3.03 us

profile of v3, /device:TPU:0, one launch (start us, length us, event | category | flops | bytes accessed | tf_op | source)
XLA Modules:
  0.0 67.2 jit_solution(6280749098343197441)
XLA Ops:
  1.3 54.6 %shard_map.247 = (bf16[256,512]{1,0:T(8,128)(2,1)}, bf16[384,512]{1,0:T(8,128)(2,1)}, f32[256,512]{1,0:T(8,128)}, f32[384,512]{1,0:T(8,128)}, f32[96,512]{1,0:T(...) custom-call(bf16[256,512]{1,0:T(8,128)(2,1)} %refs_0_.1, ...), custom_call_target="tpu_custom_call" | custom-call | tf_op jit(solution)/shard_map/pallas_call | solution.py:526
  55.9 0.0 copy-start
  55.9 1.1 %copy-done = f32[384,512]{1,0:T(8,128)S(1)} copy-done((f32[384,512]{1,0:T(8,128)S(1)}, f32[384,512]{1,0:T(8,128)}, u32[]{:S(2)}) %copy-start) | copy-done | bytes 786456
  57.0 0.0 copy-start.1
  57.0 1.0 %copy-done.1 = f32[256,512]{1,0:T(8,128)S(1)} copy-done((f32[256,512]{1,0:T(8,128)S(1)}, f32[256,512]{1,0:T(8,128)}, u32[]{:S(2)}) %copy-start.1) | copy-done | bytes 524312
  58.1 0.0 copy-start.2
  58.1 1.0 %copy-done.2 = bf16[384,512]{1,0:T(8,128)(2,1)S(1)} copy-done((bf16[384,512]{1,0:T(8,128)(2,1)S(1)}, bf16[384,512]{1,0:T(8,128)(2,1)}, u32[]{:S(2)}) %copy-start.2) | copy-done | bytes 393240
  59.1 0.0 copy-start.3
  59.1 0.9 %copy-done.3 = bf16[256,512]{1,0:T(8,128)(2,1)S(1)} copy-done((bf16[256,512]{1,0:T(8,128)(2,1)S(1)}, bf16[256,512]{1,0:T(8,128)(2,1)}, u32[]{:S(2)}) %copy-start.3) | copy-done | bytes 262168
  60.0 0.0 copy-start.4
  60.0 0.9 %copy-done.4 = f32[96,512]{1,0:T(8,128)S(1)} copy-done((f32[96,512]{1,0:T(8,128)S(1)}, f32[96,512]{1,0:T(8,128)}, u32[]{:S(2)}) %copy-start.4) | copy-done | bytes 196632
  60.9 0.0 copy-start.5
  61.0 0.9 %copy-done.5 = f32[64,512]{1,0:T(8,128)S(1)} copy-done((f32[64,512]{1,0:T(8,128)S(1)}, f32[64,512]{1,0:T(8,128)}, u32[]{:S(2)}) %copy-start.5) | copy-done | bytes 131096
  61.9 0.0 copy-start.6
  61.9 0.8 %copy-done.6 = f32[32,512]{1,0:T(8,128)S(1)} copy-done((f32[32,512]{1,0:T(8,128)S(1)}, f32[32,512]{1,0:T(8,128)}, u32[]{:S(2)}) %copy-start.6) | copy-done | bytes 65560
  62.7 0.0 copy-start.7
  62.7 0.8 %copy-done.7 = f32[32,512]{1,0:T(8,128)S(1)} copy-done((f32[32,512]{1,0:T(8,128)S(1)}, f32[32,512]{1,0:T(8,128)}, u32[]{:S(2)}) %copy-start.7) | copy-done | bytes 65560
  63.5 0.0 copy-start.8
  63.5 0.7 %copy-done.8 = f32[8,128]{1,0:T(8,128)S(1)} copy-done((f32[8,128]{1,0:T(8,128)S(1)}, f32[8,128]{1,0:T(8,128)}, u32[]{:S(2)}) %copy-start.8) | copy-done | bytes 4120
  64.2 3.0 %shard_map.248 = (bf16[256,512]{1,0:T(8,128)(2,1)}, bf16[384,512]{1,0:T(8,128)(2,1)}, f32[256,512]{1,0:T(8,128)}, f32[384,512]{1,0:T(8,128)}, f32[96,512]{1,0:T(...) custom-call(bf16[256,512]{1,0:T(8,128)(2,1)S(1)} %copy-done.3, ...), custom_call_target="tpu_custom_call" | custom-call | tf_op jit(solution)/shard_map/pallas_call | solution.py:586
Async XLA Ops:
  55.9 1.1 %copy-start = (f32[384,512]{1,0:T(8,128)S(1)}, f32[384,512]{1,0:T(8,128)}, u32[]{:S(2)}) copy-start(f32[384,512]{1,0:T(8,128)} %get-tuple-element.36.refs_3_) | copy-start | bytes 2359300
  57.0 1.0 %copy-start.1 = (f32[256,512]{1,0:T(8,128)S(1)}, f32[256,512]{1,0:T(8,128)}, u32[]{:S(2)}) copy-start(f32[256,512]{1,0:T(8,128)} %get-tuple-element.35.refs_2_) | copy-start | bytes 1572868
  58.1 1.0 %copy-start.2 = (bf16[384,512]{1,0:T(8,128)(2,1)S(1)}, bf16[384,512]{1,0:T(8,128)(2,1)}, u32[]{:S(2)}) copy-start(bf16[384,512]{1,0:T(8,128)(2,1)} %get-tuple-element.34.refs_1_) | copy-start | bytes 1179652
  59.1 0.9 %copy-start.3 = (bf16[256,512]{1,0:T(8,128)(2,1)S(1)}, bf16[256,512]{1,0:T(8,128)(2,1)}, u32[]{:S(2)}) copy-start(bf16[256,512]{1,0:T(8,128)(2,1)} %get-tuple-element.33.refs_0_) | copy-start | bytes 786436
  60.0 0.9 %copy-start.4 = (f32[96,512]{1,0:T(8,128)S(1)}, f32[96,512]{1,0:T(8,128)}, u32[]{:S(2)}) copy-start(f32[96,512]{1,0:T(8,128)} %get-tuple-element.37.refs_4_) | copy-start | bytes 589828
  60.9 0.9 %copy-start.5 = (f32[64,512]{1,0:T(8,128)S(1)}, f32[64,512]{1,0:T(8,128)}, u32[]{:S(2)}) copy-start(f32[64,512]{1,0:T(8,128)} %get-tuple-element.39.refs_6_) | copy-start | bytes 393220
  61.9 0.8 %copy-start.6 = (f32[32,512]{1,0:T(8,128)S(1)}, f32[32,512]{1,0:T(8,128)}, u32[]{:S(2)}) copy-start(f32[32,512]{1,0:T(8,128)} %get-tuple-element.38.refs_5_) | copy-start | bytes 196612
  62.7 0.8 %copy-start.7 = (f32[32,512]{1,0:T(8,128)S(1)}, f32[32,512]{1,0:T(8,128)}, u32[]{:S(2)}) copy-start(f32[32,512]{1,0:T(8,128)} %get-tuple-element.40.refs_7_) | copy-start | bytes 196612
  63.5 0.7 %copy-start.8 = (f32[8,128]{1,0:T(8,128)S(1)}, f32[8,128]{1,0:T(8,128)}, u32[]{:S(2)}) copy-start(f32[8,128]{1,0:T(8,128)} %get-tuple-element.41.refs_8_) | copy-start | bytes 12292

commit v4 on v3

--- a/solution.py
+++ b/solution.py
@@ -591,7 +591,7 @@
             out_specs=[anywhere] * len(whole) + [vmem] * 4,
             scratch_shapes=[pltpu.VMEM(array.shape, array.dtype) for array in whole]
             + [pltpu.SemaphoreType.DMA((len(whole),))] * 2,
-            compiler_params=pltpu.CompilerParams(vmem_limit_bytes=32 * 1024 * 1024),
+            compiler_params=pltpu.CompilerParams(vmem_limit_bytes=60 * 1024 * 1024),
         )(*whole, g_small)
     )
     return (

time: 67.7 us -> 60 us (0.89)
  local copies, waits for them, and re-layouts: 8.3 us -> 0 us
  Pallas kernels: 57.6 us -> 58.5 us
    unnamed x18 -> x0, local copies, waits for them, and re-layouts: 8.3 us -> none
    pallas_call x1, Pallas kernels: 3.03 us -> 3.85 us  [on_device(): pl.pallas_call(lambda *refs: copy_kernel(len(whole), *refs), out_shape=[s...]
where the time goes in v4:
time: 60 us; the launch traced here: 59.8 us
  Pallas kernels  58.5 us (98%)
  between operations  1.3 us (2%)
    pallas_call x1, Pallas kernels, on_device(): pl.pallas_call(lambda *refs: layer_kernel(peers, outer, inner, len(shares...  54.6 us
    pallas_call x1, Pallas kernels, on_device(): pl.pallas_call(lambda *refs: copy_kernel(len(whole), *refs), out_shape=[s...  3.85 us

profile of v4, /device:TPU:0, one launch (start us, length us, event | category | flops | bytes accessed | tf_op | source)
XLA Modules:
  0.0 59.8 jit_solution(11287041485938995494)
XLA Ops:
  1.3 54.6 %shard_map.247 = (bf16[256,512]{1,0:T(8,128)(2,1)}, bf16[384,512]{1,0:T(8,128)(2,1)}, f32[256,512]{1,0:T(8,128)}, f32[384,512]{1,0:T(8,128)}, f32[96,512]{1,0:T(...) custom-call(bf16[256,512]{1,0:T(8,128)(2,1)} %refs_0_.1, ...), custom_call_target="tpu_custom_call" | custom-call | tf_op jit(solution)/shard_map/pallas_call | solution.py:526
  55.9 3.9 %shard_map.248 = (bf16[256,512]{1,0:T(8,128)(2,1)}, bf16[384,512]{1,0:T(8,128)(2,1)}, f32[256,512]{1,0:T(8,128)}, f32[384,512]{1,0:T(8,128)}, f32[96,512]{1,0:T(...) custom-call(bf16[256,512]{1,0:T(8,128)(2,1)} %get-tuple-element.33.r, ...), custom_call_target="tpu_custom_call" | custom-call | tf_op jit(solution)/shard_map/pallas_call | solution.py:586
